TPU v7x, 32 devices: a whole 2x2x4 slice. The times are simulated.
32 devices in a mesh: runs: 2 (over y), lat: 4 (over z), lon: 2 (over x), lev: 2 (over core).
Axes of the slice: x: 2, y: 2, z: 4, core: 2. Of those that a mesh axis runs over, the one named last changes fastest.
Arguments:
- northward_speed: float32 [32, 128, 1792], P(('runs', 'lev'), 'lat', 'lon'), parts along dimension 0, may hold values from -6 to 6
- thermal_anomaly: float32 [32, 128, 1792], P(('runs', 'lev'), 'lat', 'lon'), parts along dimension 0, may hold values from -6 to 6
- isopycnal_bucket: int32 [32, 128, 1792], P(('runs', 'lev'), 'lat', 'lon'), parts along dimension 0, may hold values from 0 to 95
- isopycnal_bucket_slot: float32 [32, 128, 1792], P(('runs', 'lev'), 'lat', 'lon'), parts along dimension 0, may hold values from 0 to 1
- profile_region_number: int32 [256, 1792], P(('runs', 'lat'), 'lon'), parts along dimension 0, may hold values from 0 to 2, as said below
- partition_sea_lines: int32 [8, 2, 32], P(('runs', 'lat'), 'lon'), parts along dimension 0, may hold values from 0 to 31, as said below
- partition_sea_numbers: int32 [8, 2], P('runs'), parts along dimension 0, may hold values from 1 to 32, as said below
Outputs:
- depth_heat: float32 [4, 2, 16, 128], P('runs', None, 'lev', 'lat'), parts along dimension 0
- class_heat: float32 [256, 12288], P(('runs', 'lat')), parts along dimension 0
There are 2 independent parts, one for each index of `runs`. A program takes and returns all parts, laid end to end along the dimension named above; each array names one. Nothing has to cross between parts.
Inputs may be any that keep to these rules, and one draw needn't show every extreme that they name: `partition_sea_lines`: along the last dimension each device block's entries are its rows 0 to 31, each once. `partition_sea_numbers`: in every draw some device block lists all 32 of its rows. `profile_region_number`: 0 is Atlantic, 1 Indo-Pacific, 2 land; every column of a row that its device block does not list is land.
All inputs are finite; a program needn't handle non-finite values.
Results may differ from a plain program's by a relative error of at most 0.0003.
Values sent between devices are 32-bit elements; how exact they have to be, the bound alone decides.
A program may use at most 128 MiB of HBM per device.

v0:
```python
import math

import jax
import jax.numpy as jnp
from jax import lax
from jax.sharding import PartitionSpec as P

CLS = 96
TCLS = 32
NB = 2


HIGHEST = lax.Precision.HIGHEST


def eastwest_parts(zonal_sums_in, grid_point_numbers, zonal_width):
    averaging_denominator = jnp.maximum(grid_point_numbers, 1.0)[:, None, :]
    meridional_circulation_part = zonal_sums_in[0] * zonal_sums_in[1] / averaging_denominator
    stationary_eddy_part = (zonal_sums_in[2] - meridional_circulation_part) / math.sqrt(zonal_width)
    return jnp.stack(
        [
            zonal_sums_in[0] / averaging_denominator,
            zonal_sums_in[1] / averaging_denominator,
            meridional_circulation_part,
            stationary_eddy_part,
        ]
    )


def bin_blocks(device_block_list):
    quantities = device_block_list.shape[1] - 2
    block_rows = device_block_list.shape[0]
    classes = jnp.arange(CLS, dtype=jnp.float32)
    temp_classes = jnp.arange(TCLS, dtype=jnp.float32)
    class_pos = device_block_list[:, quantities, :]
    temp_pos = device_block_list[:, quantities + 1, :]
    tent_weights = jnp.maximum(0.0, 1.0 - jnp.abs(class_pos[:, None, :] - classes[None, :, None]))
    temp_weights = jnp.maximum(
        0.0, 1.0 - jnp.abs(temp_pos[:, None, :] - temp_classes[None, :, None])
    )
    weighted = (device_block_list[:, :quantities, None, :] * temp_weights[:, None]).reshape(
        block_rows, quantities * TCLS, -1
    )
    class_binned_heat = jnp.einsum("gml,gcl->gmc", weighted, tent_weights, precision=HIGHEST)
    return class_binned_heat.reshape(block_rows, quantities * TCLS * CLS)


def class_tally(device_block_list, row_ordering, wet_cell_total):
    slot_count = device_block_list.shape[0]
    out_width = (device_block_list.shape[1] - 2) * TCLS * CLS
    targets = jnp.arange(slot_count, dtype=jnp.int32)

    def turn_step(step_index, running):
        offset = 2 * step_index
        chosen_rows = lax.dynamic_slice_in_dim(row_ordering, offset, 2)
        is_live = (offset + jnp.arange(2, dtype=jnp.int32) < wet_cell_total).astype(jnp.float32)
        class_binned_heat = bin_blocks(jnp.take(device_block_list, chosen_rows, axis=0))
        matches = (chosen_rows[:, None] == targets[None, :]).astype(jnp.float32) * is_live[:, None]
        return running + jnp.dot(matches.T, class_binned_heat, precision=HIGHEST)

    return lax.fori_loop(
        0, (wet_cell_total + 1) // 2, turn_step, jnp.zeros((slot_count, out_width), jnp.float32)
    )


def shards(
    northward_speed,
    thermal_anomaly,
    isopycnal_bucket,
    isopycnal_bucket_slot,
    profile_region_number,
    partition_sea_lines,
    partition_sea_numbers,
):
    depth_level_list, row_count, col_count = northward_speed.shape
    zonal_width = col_count * lax.axis_size("lon")
    level_count = depth_level_list * lax.axis_size("lev")
    basins = jnp.arange(NB, dtype=jnp.int32)
    ocean_region_filters = (profile_region_number[None] == basins[:, None, None]).astype(
        jnp.float32
    )
    northward_filtered = ocean_region_filters[:, None] * northward_speed[None]
    stacked = jnp.stack(
        [
            jnp.sum(northward_filtered, -1),
            jnp.sum(ocean_region_filters[:, None] * thermal_anomaly[None], -1),
            jnp.sum(northward_filtered * thermal_anomaly[None], -1),
        ]
    )
    local_counts = jnp.sum(ocean_region_filters, -1)
    total_sums, total_counts = lax.psum((stacked, local_counts), "lon")
    eastwest_moments = eastwest_parts(total_sums, total_counts, zonal_width)
    northward_departure = northward_speed[None] - eastwest_moments[0][..., None]
    thermal_departure = thermal_anomaly[None] - eastwest_moments[1][..., None]
    features = jnp.concatenate(
        [
            northward_filtered,
            ocean_region_filters[:, None] * northward_departure * thermal_departure,
        ],
        0,
    )
    quantities = features.shape[0]
    cell_width = depth_level_list * col_count
    class_pos = jnp.minimum(isopycnal_bucket.astype(jnp.float32) + isopycnal_bucket_slot, CLS - 1.0)
    temp_pos = jnp.minimum(jnp.maximum((thermal_anomaly + 3.0) * (TCLS / 6.0), 0.0), TCLS - 1.0)
    payload = jnp.concatenate([features, class_pos[None], temp_pos[None]], 0)
    payload = jnp.transpose(payload, (2, 0, 1, 3)).reshape(row_count, quantities + 2, cell_width)
    listing = partition_sea_lines[0, 0]
    own_count = partition_sea_numbers[lax.axis_index("lat"), lax.axis_index("lon")]
    row_rank = jnp.sum(
        (listing[None, :] == jnp.arange(row_count, dtype=jnp.int32)[:, None])
        * jnp.arange(row_count, dtype=jnp.int32)[None, :],
        axis=1,
    )
    band_count = lax.axis_size("lat")
    my_band = lax.axis_index("lat")
    per_band = row_count // band_count
    slot_pos = (
        jnp.arange(per_band, dtype=jnp.int32)[None, :] * band_count
        + (jnp.arange(band_count, dtype=jnp.int32)[:, None] - my_band) % band_count
    )
    is_live = slot_pos < own_count
    outgoing = jnp.take(payload, listing[slot_pos], axis=0)
    marker = jnp.concatenate(
        [
            jnp.zeros((quantities, cell_width), jnp.float32),
            jnp.full((1, cell_width), -2.0, jnp.float32),
            jnp.zeros((1, cell_width), jnp.float32),
        ],
        0,
    )
    outgoing = jnp.where(is_live[:, :, None, None], outgoing, marker[None, None])
    arrived = lax.all_to_all(outgoing, "lat", split_axis=0, concat_axis=0, tiled=True)
    senders = arrived.shape[0]
    item_count = arrived.shape[1]
    flattened_cells = arrived.reshape(senders * item_count, quantities + 2, cell_width)
    valid_cell_mask = flattened_cells[:, quantities, 0] >= 0.0
    sort_keys = jnp.where(valid_cell_mask, 0, senders * item_count) + jnp.arange(
        senders * item_count, dtype=jnp.int32
    )
    row_ordering = jnp.argsort(sort_keys)
    class_binned_heat = class_tally(
        flattened_cells, row_ordering, jnp.sum(valid_cell_mask.astype(jnp.int32))
    )
    answers = lax.all_to_all(
        class_binned_heat.reshape(senders, item_count, quantities * TCLS * CLS),
        "lat",
        split_axis=0,
        concat_axis=0,
        tiled=True,
    )
    flat_slot = (my_band + row_rank) % band_count * per_band + row_rank // band_count
    matches = (
        flat_slot[:, None] == jnp.arange(band_count * per_band, dtype=jnp.int32)[None, :]
    ) & (row_rank < own_count)[:, None]
    totals = jnp.dot(
        matches.astype(jnp.float32),
        answers.reshape(band_count * per_band, quantities * TCLS * CLS),
        precision=HIGHEST,
    )
    class_heat = lax.psum(totals, ("lon", "lev")) / math.sqrt(
        level_count * zonal_width / (CLS * TCLS)
    )
    return (eastwest_moments[2:], class_heat)


def solution(mesh):
    in_specs = (
        P(("runs", "lev"), "lat", "lon"),
        P(("runs", "lev"), "lat", "lon"),
        P(("runs", "lev"), "lat", "lon"),
        P(("runs", "lev"), "lat", "lon"),
        P(("runs", "lat"), "lon"),
        P(("runs", "lat"), "lon", None),
        P("runs", None),
    )
    out_specs = (P("runs", None, "lev", "lat"), P(("runs", "lat"), None))
    return jax.shard_map(shards, mesh=mesh, in_specs=in_specs, out_specs=out_specs, check_vma=False)
```

profile of v0, /device:TPU:0, one launch (start us, length us, event | category | flops | bytes accessed | tf_op | source)
XLA Modules:
  0.0 436.4 jit_solution(11052665706332396745)
XLA Ops:
  12.6 10.1 %all-reduce = (f32[3,2,8,32]{3,2,1,0:T(8,128)S(1)}, f32[2,32]{1,0:T(2,128)S(1)}) all-reduce(f32[3,2,8,32]{3,2,1,0:T(8,128)S(1)} %pad_maximum_fusion, f32[2,32]{1,0:T(2,128)S(1)} %fusion.22), channel_id=1, replica_groups=mesh['runs'=2,'lat'=4,'lon'=2,'lev'=2] {'lon'}, use_global_device_ids=true, to_apply=%region_3.0 | all-reduce | flops 1600 | bytes 12800 | tf_op jit(solution)/shard_map/psum | solution.py:91
  28.7 6.8 %reshape.227 = f32[32,6,7168]{2,0,1:T(8,128)} reshape(f32[32,6,8,896]{3,2,0,1:T(8,128)} %maximum_bitcast_fusion) | data formatting | bytes 11010048 | tf_op jit(solution)/shard_map/reshape | solution.py:107
  35.4 8.8 %copy.67 = f32[32,6,7168]{2,1,0:T(8,128)} copy(f32[32,6,7168]{2,0,1:T(8,128)} %reshape.227) | data formatting | bytes 11010048 | tf_op jit(solution)/shard_map/reshape | solution.py:107
  45.6 7.2 %gather_fusion.2 = f32[32,6,7168]{2,1,0:T(8,128)} fusion(f32[32,6,7168]{2,1,0:T(8,128)} %copy.67, s32[1024]{0:T(1024)S(1)} %pad_clamp_fusion.1), kind=kCustom, calls=%fused_computation.2 | custom fusion | bytes 11010176 | tf_op jit(solution)/shard_map/jit(_take)/gather | solution.py:123
  52.8 8.9 %fusion.18 = f32[4,8,6,7168]{3,1,2,0:T(8,128)} fusion(f32[4,8,6,7168]{3,2,1,0:T(8,128)} %bitcast.53, f32[6,7168]{1,0:T(8,128)S(1)} %copy-done.4, pred[4,8]{1,0:T(4,128)(4,1)S(1)} %get-tuple-element.111, pred[4,8]{1,0:T(4,128)(4,1)S(1)} %get-tuple-element.110), kind=kLoop, calls=%fused_computation.34 | loop fusion | flops 2752512 | bytes 11182144 | tf_op jit(solution)/shard_map/jit(_where)/select_n | solution.py:132
  61.7 5.3 %all-to-all-start = ((f32[4,8,6,7168]{3,1,2,0:T(8,128)}), f32[4,8,6,7168]{3,1,2,0:T(8,128)}, u32[]{:S(2)}, u32[]{:S(2)}) async-start(f32[4,8,6,7168]{3,1,2,0:T(8,128)} %fusion.18), calls=%async_computation | async-start | bytes 11010048 | tf_op jit(solution)/shard_map/all_to_all | solution.py:133
  67.0 119.4 %all-to-all-done = f32[4,8,6,7168]{3,1,2,0:T(8,128)} async-done(((f32[4,8,6,7168]{3,1,2,0:T(8,128)}), f32[4,8,6,7168]{3,1,2,0:T(8,128)}, u32[]{:S(2)}, u32[]{:S(2)}) %all-to-all-start) | async-done | bytes 5505056 | tf_op jit(solution)/shard_map/all_to_all | solution.py:133
  193.3 8.8 %copy.70 = f32[32,6,7168]{2,1,0:T(8,128)} copy(f32[32,6,7168]{2,0,1:T(8,128)} %bitcast.55) | data formatting | bytes 11010048
  205.0 122.0 %while.11 = (s32[]{:T(128)}, f32[32,12288]{1,0:T(8,128)}, s32[]{:T(128)}, s32[32]{0:T(128)S(1)}, s32[]{:T(128)}, /*index=5*/f32[32,6,7168]{2,1,0:T(8,128)}, s32[]{:T(128)}, s32[]{:T(128)}, s32[]{:T(128)}, s32[]{:T(128)}) while((s32[]{:T(128)}, f32[32,12288]{1,0:T(8,128)}, s32[]{:T(128)}, s32[32]{0:T(128)S(1)}, s32[]{:T(128)}, ...), condition=%wide.region_10.11_spmd.clone, body=%wide.region_9.10_spmd.clone.sunk | while | flops 2133021824 | bytes 24531180 | solution.py:61
  210.9 7.3 %fusion.44 = f32[2,128,96]{2,1,0:T(8,128)S(1)} fusion(f32[2,128,7168]{2,1,0:T(8,128)S(1)} %bitcast.52, f32[2,7168]{1,0:T(2,128)S(1)} %bitcast.57), kind=kOutput, calls=%fused_computation.5.clone.1 | convolution fusion | flops 2119434240 | bytes 7495680 | tf_op jit(solution)/shard_map/while/body/gml,gcl->gmc/dot_general | solution.py:44
  218.4 4.1 convolution_add_fusion.2
  228.3 7.3 %fusion.44 = f32[2,128,96]{2,1,0:T(8,128)S(1)} fusion(f32[2,128,7168]{2,1,0:T(8,128)S(1)} %bitcast.52, f32[2,7168]{1,0:T(2,128)S(1)} %bitcast.57), kind=kOutput, calls=%fused_computation.5.clone.1 | convolution fusion | flops 2119434240 | bytes 7495680 | tf_op jit(solution)/shard_map/while/body/gml,gcl->gmc/dot_general | solution.py:44
  235.8 4.1 convolution_add_fusion.2
  245.8 7.3 %fusion.44 = f32[2,128,96]{2,1,0:T(8,128)S(1)} fusion(f32[2,128,7168]{2,1,0:T(8,128)S(1)} %bitcast.52, f32[2,7168]{1,0:T(2,128)S(1)} %bitcast.57), kind=kOutput, calls=%fused_computation.5.clone.1 | convolution fusion | flops 2119434240 | bytes 7495680 | tf_op jit(solution)/shard_map/while/body/gml,gcl->gmc/dot_general | solution.py:44
  253.2 4.1 convolution_add_fusion.2
  263.2 7.3 %fusion.44 = f32[2,128,96]{2,1,0:T(8,128)S(1)} fusion(f32[2,128,7168]{2,1,0:T(8,128)S(1)} %bitcast.52, f32[2,7168]{1,0:T(2,128)S(1)} %bitcast.57), kind=kOutput, calls=%fused_computation.5.clone.1 | convolution fusion | flops 2119434240 | bytes 7495680 | tf_op jit(solution)/shard_map/while/body/gml,gcl->gmc/dot_general | solution.py:44
  280.6 7.3 %fusion.44 = f32[2,128,96]{2,1,0:T(8,128)S(1)} fusion(f32[2,128,7168]{2,1,0:T(8,128)S(1)} %bitcast.52, f32[2,7168]{1,0:T(2,128)S(1)} %bitcast.57), kind=kOutput, calls=%fused_computation.5.clone.1 | convolution fusion | flops 2119434240 | bytes 7495680 | tf_op jit(solution)/shard_map/while/body/gml,gcl->gmc/dot_general | solution.py:44
  288.1 4.1 convolution_add_fusion.2
  298.0 7.3 %fusion.44 = f32[2,128,96]{2,1,0:T(8,128)S(1)} fusion(f32[2,128,7168]{2,1,0:T(8,128)S(1)} %bitcast.52, f32[2,7168]{1,0:T(2,128)S(1)} %bitcast.57), kind=kOutput, calls=%fused_computation.5.clone.1 | convolution fusion | flops 2119434240 | bytes 7495680 | tf_op jit(solution)/shard_map/while/body/gml,gcl->gmc/dot_general | solution.py:44
  305.5 4.1 convolution_add_fusion.2
  315.5 7.3 %fusion.44 = f32[2,128,96]{2,1,0:T(8,128)S(1)} fusion(f32[2,128,7168]{2,1,0:T(8,128)S(1)} %bitcast.52, f32[2,7168]{1,0:T(2,128)S(1)} %bitcast.57), kind=kOutput, calls=%fused_computation.5.clone.1 | convolution fusion | flops 2119434240 | bytes 7495680 | tf_op jit(solution)/shard_map/while/body/gml,gcl->gmc/dot_general | solution.py:44
  322.9 4.1 convolution_add_fusion.2
  331.5 35.6 %all-to-all-done.1 = f32[4,8,12288]{2,1,0:T(8,128)S(1)} async-done(((f32[4,8,12288]{2,1,0:T(8,128)}), f32[4,8,12288]{2,1,0:T(8,128)S(1)}, u32[]{:S(2)}, u32[]{:S(2)}) %all-to-all-start.1) | async-done | bytes 1572896 | tf_op jit(solution)/shard_map/all_to_all | solution.py:145
  369.8 57.1 %all-reduce.3.cloned.1.call-done = f32[32,12288]{1,0:T(8,128)} async-done(((f32[32,12288]{1,0:T(8,128)}), f32[32,12288]{1,0:T(8,128)}) %all-reduce.3.cloned.1.call-update) | async-done | bytes 1572880 | tf_op jit(solution)/shard_map/psum | solution.py:161
  (145 shorter events, 77.6 us)
Async XLA Ops:
  7.2 1.9 copy-start.3
  7.2 2.0 copy-start.2
  35.4 8.9 %copy-start.5 = (s32[4,2]{0,1:T(2,128)S(1)}, s32[4,2]{0,1:T(2,128)}, u32[]{:S(2)}) copy-start(s32[4,2]{0,1:T(2,128)} %param.15) | copy-start | bytes 100
  45.6 7.2 %copy-start.4 = (f32[6,7168]{1,0:T(8,128)S(1)}, f32[6,7168]{1,0:T(8,128)}, u32[]{:S(2)}) copy-start(f32[6,7168]{1,0:T(8,128)} %constant.131.clone.1) | copy-start | bytes 516100
  61.7 124.8 %all-to-all-start = ((f32[4,8,6,7168]{3,1,2,0:T(8,128)}), f32[4,8,6,7168]{3,1,2,0:T(8,128)}, u32[]{:S(2)}, u32[]{:S(2)}) async-start(f32[4,8,6,7168]{3,1,2,0:T(8,128)} %fusion.18), calls=%async_computation | async-start | bytes 11010048 | tf_op jit(solution)/shard_map/all_to_all | solution.py:133
  189.5 2.4 copy-start.1
  327.0 3.8 copy-start
  327.0 40.1 %all-to-all-start.1 = ((f32[4,8,12288]{2,1,0:T(8,128)}), f32[4,8,12288]{2,1,0:T(8,128)S(1)}, u32[]{:S(2)}, u32[]{:S(2)}) async-start(f32[4,8,12288]{2,1,0:T(8,128)} %bitcast.12), calls=%async_computation.1 | async-start | bytes 3145728 | tf_op jit(solution)/shard_map/all_to_all | solution.py:145
  330.7 96.2 %all-reduce.3.cloned.1.call-start = ((), (), s32[]{:S(2)}) async-start(), calls=%async_computation.2 | async-start | bytes 3145728 | tf_op jit(solution)/shard_map/psum | solution.py:161
Sparse Core Ops, SparseCore 0:
  369.3 57.5 all-reduce.2
where the time goes:
time: 429 us; the launch traced here: 436 us
  waiting for transfers between devices  212 us (49%)
  matrix products  81.5 us (19%)
  local copies, waits for them, and re-layouts  72.7 us (17%)
  other arithmetic  35.6 us (8%)
  between operations  14.9 us (3%)
  blocking collectives  10.1 us (2%)
  starting transfers between devices  9.08 us (2%)
    all_to_all x1, waiting for transfers between devices, shards(): lax.all_to_all(outgoing, 'lat', split_axis=0, concat_axis=0, tiled=True)  119 us
    psum x1, waiting for transfers between devices, shards(): lax.psum(totals, ('lon', 'lev'))  57.1 us
    dot_general x7, matrix products, bin_blocks(): jnp.einsum('gml,gcl->gmc', weighted, tent_weights, precision=HIGHEST)  50.9 us
    all_to_all x1, waiting for transfers between devices, shards(): lax.all_to_all(class_binned_heat.reshape(senders, item_count, quantities...  35.6 us
    dot_general x7, matrix products, turn_step(): return running + jnp.dot(matches.T, class_binned_heat, precision=HIGHEST)  28.5 us
    gather x7, local copies, waits for them, and re-layouts, turn_step(): jnp.take(device_block_list, chosen_rows, axis=0)  25.6 us
    reshape x2, local copies, waits for them, and re-layouts, shards(): jnp.transpose(payload, (2, 0, 1, 3))  15.6 us
    unnamed x15, local copies, waits for them, and re-layouts  13.5 us
  transfers between devices with their start and end apart: 3, of which 3 were waited for; matrix products, arithmetic and copies ran while one was open for 0% of the time, Pallas kernels for 0%

commit v1 on v0

v1 whole, which is shorter than its diff:
```python
import functools
import math

import jax
import jax.numpy as jnp
from jax import lax
from jax.experimental import pallas as pl
from jax.experimental.pallas import tpu as pltpu
from jax.sharding import PartitionSpec as P

CLS = 96
TCLS = 32
NB = 2
BT = NB * TCLS
QT = 2 * BT
F32 = jnp.float32
BF16 = jnp.bfloat16


def split(x):
    high = x.astype(BF16).astype(F32)
    return high, x - high


def prepare(k, v, t, bucket, slot, basin, means, rows_ref):
    position = jnp.minimum(bucket.astype(F32) + slot, CLS - 1.0)
    cls = jnp.floor(position)
    upper = position - cls
    temp_pos = jnp.minimum(jnp.maximum((t + 3.0) * (TCLS / 6.0), 0.0), TCLS - 1.0)
    temp = jnp.floor(temp_pos)
    warm = temp_pos - temp
    cold = 1.0 - warm
    first = basin == 0
    second = basin == 1
    mean_v = jnp.where(first, means[0], means[1])
    mean_t = jnp.where(first, means[2], means[3])
    eddy = (v - mean_v) * (t - mean_t)
    joint = jnp.where(first, temp, jnp.where(second, temp + TCLS, -128.0))
    values = [cls, *split(1.0 - upper), *split(upper), joint]
    for feature in (v, eddy):
        values += [*split(feature * cold), *split(feature * warm)]
    for slot_at, value in enumerate(values):
        rows_ref[slot_at, k] = value


def bin_row(y, rows_ref, levels, columns, scale):
    spots = lax.broadcasted_iota(jnp.int32, (16, columns), 0).astype(F32)
    total = None
    step = 2 if levels % 2 == 0 else 1
    for k0 in range(0, levels, step):
        tents, weights = [], []
        for k in range(k0, k0 + step):
            def row(at):
                return jnp.broadcast_to(rows_ref[at, k, pl.ds(y, 1), :], (16, columns)).astype(BF16)

            zero = jnp.zeros((16, columns), BF16)
            cls, low_hi, low_lo, up_hi, up_lo, joint = [row(at) for at in range(6)]
            feats = [row(at) for at in range(6, 14)]
            tent_hi, tent_lo = [], []
            for c in range(0, CLS, 16):
                here = (spots + float(c)).astype(BF16)
                before = (spots + float(c - 1)).astype(BF16)
                at_low = cls == here
                at_up = cls == before
                tent_hi.append(jnp.where(at_low, low_hi, jnp.where(at_up, up_hi, zero)))
                tent_lo.append(jnp.where(at_low, low_lo, jnp.where(at_up, up_lo, zero)))
            blocks = [[], [], [], []]
            for c in range(0, BT, 16):
                here = (spots + float(c)).astype(BF16)
                before = (spots + float(c - 1)).astype(BF16)
                at_low = joint == here
                at_up = joint == before
                for n, (kind, part) in enumerate(((0, 0), (1, 0), (0, 1), (1, 1))):
                    low = feats[4 * kind + part]
                    up = feats[4 * kind + 2 + part]
                    blocks[n].append(jnp.where(at_low, low, jnp.where(at_up, up, zero)))
            tents.append(jnp.concatenate(tent_hi + tent_lo, 0))
            weights.append(jnp.concatenate(sum(blocks, []), 0))
        product = lax.dot_general(
            jnp.concatenate(tents, 1),
            jnp.concatenate(weights, 1),
            (((1,), (1,)), ((), ())),
            preferred_element_type=F32,
        )
        total = product if total is None else total + product
    total = total[:, :QT] + total[:, QT:]
    return (total[:CLS] + total[CLS:]) * scale


def bin_kernel(scale, v_ref, t_ref, bucket_ref, slot_ref, basin_ref, means_ref, out_ref, rows_ref, sums_ref):
    levels, row_count, columns = v_ref.shape
    basin = basin_ref[...]
    for k in range(levels):
        means = [means_ref[:, 4 * k + n : 4 * k + n + 1] for n in range(4)]
        prepare(k, v_ref[k], t_ref[k], bucket_ref[k], slot_ref[k], basin, means, rows_ref)

    def one_row(y, carry):
        binned = bin_row(y, rows_ref, levels, columns, scale)
        binned = jnp.concatenate([binned, jnp.zeros((128 - CLS, QT), F32)], 0)
        sums_ref[pl.ds(y, QT, stride=row_count), :] = binned.T
        return carry

    lax.fori_loop(0, row_count, one_row, 0)

    def flatten(group, carry):
        parts = []
        for m in range(4):
            start = pl.multiple_of((group * 4 + m) * row_count, row_count)
            parts.append(sums_ref[pl.ds(start, row_count), :][:, :CLS])
        out_ref[:, pl.ds(pl.multiple_of(group * (4 * CLS), 128), 4 * CLS)] = jnp.concatenate(parts, 1)
        return carry

    lax.fori_loop(0, QT // 4, flatten, 0)


def shards(
    northward_speed,
    thermal_anomaly,
    isopycnal_bucket,
    isopycnal_bucket_slot,
    profile_region_number,
    partition_sea_lines,
    partition_sea_numbers,
):
    levels, row_count, columns = northward_speed.shape
    zonal_width = columns * lax.axis_size("lon")
    level_count = levels * lax.axis_size("lev")
    basins = jnp.arange(NB, dtype=jnp.int32)
    masks = (profile_region_number[None] == basins[:, None, None]).astype(F32)
    filtered = masks[:, None] * northward_speed[None]
    stacked = jnp.stack(
        [
            jnp.sum(filtered, -1),
            jnp.sum(masks[:, None] * thermal_anomaly[None], -1),
            jnp.sum(filtered * thermal_anomaly[None], -1),
        ]
    )
    sums, counts = lax.psum((stacked, jnp.sum(masks, -1)), "lon")
    divisor = jnp.maximum(counts, 1.0)[:, None, :]
    means = sums[:2] / divisor
    overturning = sums[0] * sums[1] / divisor
    eddy = (sums[2] - overturning) / math.sqrt(zonal_width)
    depth_heat = jnp.stack([overturning, eddy])
    own_count = partition_sea_numbers[lax.axis_index("lat"), lax.axis_index("lon")]
    lines = partition_sea_lines[0, 0]
    places = jnp.arange(row_count, dtype=jnp.int32)
    listed = jnp.any((lines[None, :] == places[:, None]) & (places[None, :] < own_count), 1)
    basin = jnp.where(listed[:, None], profile_region_number, NB)
    means = jnp.transpose(means, (3, 2, 0, 1)).reshape(row_count, levels * 4)
    means = jnp.pad(means, ((0, 0), (0, 128 - levels * 4)))
    scale = 1.0 / math.sqrt(level_count * zonal_width / (CLS * TCLS))
    vmem = pl.BlockSpec(memory_space=pltpu.VMEM)
    binned = pl.pallas_call(
        functools.partial(bin_kernel, scale),
        out_shape=jax.ShapeDtypeStruct((row_count, QT * CLS), F32),
        in_specs=[vmem] * 6,
        out_specs=vmem,
        scratch_shapes=[
            pltpu.VMEM((14, levels, row_count, columns), F32),
            pltpu.VMEM((QT * row_count, 128), F32),
        ],
        compiler_params=pltpu.CompilerParams(vmem_limit_bytes=48 * 1024 * 1024),
    )(northward_speed, thermal_anomaly, isopycnal_bucket, isopycnal_bucket_slot, basin, means)
    return depth_heat, lax.psum(binned, ("lon", "lev"))


def solution(mesh):
    in_specs = (
        P(("runs", "lev"), "lat", "lon"),
        P(("runs", "lev"), "lat", "lon"),
        P(("runs", "lev"), "lat", "lon"),
        P(("runs", "lev"), "lat", "lon"),
        P(("runs", "lat"), "lon"),
        P(("runs", "lat"), "lon", None),
        P("runs", None),
    )
    out_specs = (P("runs", None, "lev", "lat"), P(("runs", "lat"), None))
    return jax.shard_map(shards, mesh=mesh, in_specs=in_specs, out_specs=out_specs, check_vma=False)
```

time: 429 us -> 132 us (0.31); the launches traced: 436 us -> 131 us
  waiting for transfers between devices: 212 us -> 42.6 us
  matrix products: 81.5 us -> 0 us
  local copies, waits for them, and re-layouts: 72.7 us -> 5.2 us
  Pallas kernels: 0 us -> 52.4 us
  other arithmetic: 35.6 us -> 7.15 us
  starting transfers between devices: 9.08 us -> 0.04 us
    all_to_all x2 -> x0, waiting for transfers between devices: 155 us -> none  [the longest x1 119 us: shards(): lax.all_to_all(outgoing, 'lat', split_axis=0, concat_axis=0, tiled=True)]
    dot_general x15 -> x0, matrix products: 81.5 us -> none  [the longest x7 50.9 us: bin_blocks(): jnp.einsum('gml,gcl->gmc', weighted, tent_weights, precision=HIGHEST)]
    pallas_call x0 -> x1, Pallas kernels: none -> 52.4 us  [shards(): pl.pallas_call(functools.partial(bin_kernel, scale), out_shape=jax.ShapeD...]
    gather x11 -> x0, local copies, waits for them, and re-layouts: 34.4 us -> none  [the longest x7 25.6 us: turn_step(): jnp.take(device_block_list, chosen_rows, axis=0)]
    reshape x9 -> x1, local copies, waits for them, and re-layouts: 16.8 us -> 0.07 us  [shards(): means = jnp.transpose(means, (3, 2, 0, 1)).reshape(row_count, levels * 4)]
    psum x1, waiting for transfers between devices: 57.1 us -> 42.6 us  [shards(): return (depth_heat, lax.psum(binned, ('lon', 'lev')))]
    unnamed x15 -> x9, local copies, waits for them, and re-layouts: 13.5 us -> 3.84 us
    select_n x19 -> x1, other arithmetic: 10.5 us -> 0.98 us  [shards(): basin = jnp.where(listed[:, None], profile_region_number, NB)]
  transfers between devices with their start and end apart: 3 -> 1, of which waited for: 3 -> 1; matrix products, arithmetic and copies ran while one was open for 0% -> 0% of each run, Pallas kernels for 0% -> 0%
where the time goes in v1:
time: 132 us; the launch traced here: 131 us
  Pallas kernels  52.4 us (40%)
  waiting for transfers between devices  42.6 us (32%)
  between operations  14.1 us (11%)
  blocking collectives  9.93 us (8%)
  other arithmetic  7.15 us (5%)
  local copies, waits for them, and re-layouts  5.2 us (4%)
    pallas_call x1, Pallas kernels, shards(): pl.pallas_call(functools.partial(bin_kernel, scale), out_shape=jax.ShapeD...  52.4 us
    psum x1, waiting for transfers between devices, shards(): return (depth_heat, lax.psum(binned, ('lon', 'lev')))  42.6 us
    psum x1, blocking collectives, shards(): sums, counts = lax.psum((stacked, jnp.sum(masks, -1)), 'lon')  9.93 us
    unnamed x9, local copies, waits for them, and re-layouts  3.84 us
  transfers between devices with their start and end apart: 1, of which 1 were waited for; matrix products, arithmetic and copies ran while one was open for 0% of the time, Pallas kernels for 0%

profile of v1, /device:TPU:0, one launch (start us, length us, event | category | flops | bytes accessed | tf_op | source)
XLA Modules:
  0.0 131.4 jit_solution(14490254276671086763)
XLA Ops:
  7.2 0.0 copy-start.1
  7.2 0.0 copy-start
  7.2 0.0 copy-start.2
  7.2 0.0 all-reduce.4.cloned.1.call-start
  7.2 1.2 fusion.2
  8.4 0.9 fusion.1
  9.3 1.3 dynamic_slice.3
  10.6 0.6 iota_compare_fusion.2
  11.3 0.8 fusion.5
  12.0 1.0 broadcast_select_fusion.basin_ref
  13.0 2.0 %multiply_reduce_fusion = (f32[2,8,32]{2,1,0:T(8,128)S(1)}, f32[2,8,32]{2,1,0:T(8,128)S(1)}, f32[2,8,32]{2,1,0:T(8,128)S(1)}) fusion(f32[8,32,896]{2,1,0:T(8,128)} %v_ref.1, f32[2,32,896]{2,1,0:T(8,128)S(1)} %fusion.1, f32[8,32,896]{2,1,0:T(8,128)} %t_ref.1), kind=kLoop, calls=%fused_computation.1 | loop fusion | flops 2750976 | bytes 2070528 | tf_op jit(solution)/shard_map/reduce_sum | solution.py:133
  15.1 9.9 %all-reduce.1 = (f32[3,2,8,32]{3,2,1,0:T(8,128)S(1)}, f32[2,32]{1,0:T(2,128)S(1)}) all-reduce(f32[3,2,8,32]{3,2,1,0:T(8,128)S(1)} %pad_maximum_fusion, f32[2,32]{1,0:T(2,128)S(1)} %fusion.2), channel_id=1, replica_groups=mesh['runs'=2,'lat'=4,'lon'=2,'lev'=2] {'lon'}, use_global_device_ids=true, to_apply=%region_3.0 | all-reduce | flops 1600 | bytes 12800 | tf_op jit(solution)/shard_map/psum | solution.py:138
  25.0 0.1 copy.13
  25.1 0.0 copy-done.1
  25.1 0.0 copy-done
  25.1 0.0 copy-done.2
  25.1 0.0 copy-start.3
  25.1 1.2 copy-done.3
  26.3 52.4 %shard_map.86 = f32[32,12288]{1,0:T(8,128)} custom-call(f32[8,32,896]{2,1,0:T(8,128)S(1)} %copy-done, f32[8,32,896]{2,1,0:T(8,128)S(1)} %copy-done.1, s32[8,32,896]{2,1,0:T(8,128)S(1)} %copy-done.2, f32[8,32,896]{2,1,0:T(8,128)S(1)} %copy-done.3, s32[32,896]{1,0:T(8,128)S(1)} %broadcast_select_fusion.basin_ref, f32[32,128]{1,0:T(8,128)S(1)} %pad.4.means_ref), custom_call_target="tpu_custom_call" | custom-call | tf_op jit(solution)/shard_map/pallas_call | solution.py:153
  78.7 0.0 all-reduce.4.cloned.1.call-update
  78.7 0.6 pad_maximum_fusion.1
  79.3 42.6 %all-reduce.4.cloned.1.call-done = f32[32,12288]{1,0:T(8,128)} async-done(((f32[32,12288]{1,0:T(8,128)}), f32[32,12288]{1,0:T(8,128)}) %all-reduce.4.cloned.1.call-update) | async-done | bytes 1572880 | tf_op jit(solution)/shard_map/psum | solution.py:164
  121.9 2.7 %copy.15 = f32[32,12288]{1,0:T(8,128)} copy(f32[32,12288]{1,0:T(8,128)} %all-reduce.4.cloned.1.call-done) | data formatting | bytes 3145728
  (6 shorter events, 0.0 us)
Async XLA Ops:
  7.2 17.9 %copy-start.1 = (f32[8,32,896]{2,1,0:T(8,128)S(1)}, f32[8,32,896]{2,1,0:T(8,128)}, u32[]{:S(2)}) copy-start(f32[8,32,896]{2,1,0:T(8,128)} %t_ref.1) | copy-start | bytes 2752516
  7.2 17.9 %copy-start = (f32[8,32,896]{2,1,0:T(8,128)S(1)}, f32[8,32,896]{2,1,0:T(8,128)}, u32[]{:S(2)}) copy-start(f32[8,32,896]{2,1,0:T(8,128)} %v_ref.1) | copy-start | bytes 2752516
  7.2 17.9 %copy-start.2 = (s32[8,32,896]{2,1,0:T(8,128)S(1)}, s32[8,32,896]{2,1,0:T(8,128)}, u32[]{:S(2)}) copy-start(s32[8,32,896]{2,1,0:T(8,128)} %bucket_ref.1) | copy-start | bytes 2752516
  7.2 114.7 %all-reduce.4.cloned.1.call-start = ((), (), s32[]{:S(2)}) async-start(), calls=%async_computation | async-start | bytes 3145728 | tf_op jit(solution)/shard_map/psum | solution.py:164
  25.1 1.2 copy-start.3
Sparse Core Ops, SparseCore 0:
  78.8 43.0 all-reduce.3

commit v2 on v1

v2 whole, which is shorter than its diff:
```python
import functools
import math

import jax
import jax.numpy as jnp
from jax import lax
from jax.experimental import pallas as pl
from jax.experimental.pallas import tpu as pltpu
from jax.sharding import PartitionSpec as P

CLS = 96
TCLS = 32
NB = 2
BT = NB * TCLS
QT = 2 * BT
F32 = jnp.float32
BF16 = jnp.bfloat16


def split(x):
    high = x.astype(BF16).astype(F32)
    return high, x - high


ROWS = 8
STATS = 8


def temperature(t):
    temp_pos = jnp.minimum(jnp.maximum((t + 3.0) * (TCLS / 6.0), 0.0), TCLS - 1.0)
    temp = jnp.floor(temp_pos)
    return temp, temp_pos - temp


def prepare_classes(k, v, t, bucket, slot, listed_basin, rows_ref):
    position = jnp.minimum(bucket.astype(F32) + slot, CLS - 1.0)
    cls = jnp.floor(position)
    upper = position - cls
    temp, warm = temperature(t)
    joint = jnp.where(
        listed_basin == 0, temp, jnp.where(listed_basin == 1, temp + TCLS, -128.0)
    )
    values = [cls, *split(1.0 - upper), *split(upper), joint]
    values += [*split(v * (1.0 - warm)), *split(v * warm)]
    for at, value in enumerate(values):
        rows_ref[at, k] = value


def prepare_eddies(k, v, t, listed_basin, means, rows_ref):
    first = listed_basin == 0
    eddy = (v - jnp.where(first, means[0], means[1])) * (t - jnp.where(first, means[2], means[3]))
    _, warm = temperature(t)
    for at, value in enumerate([*split(eddy * (1.0 - warm)), *split(eddy * warm)]):
        rows_ref[10 + at, k] = value


def bin_row(y, rows_ref, levels, columns, scale):
    spots = lax.broadcasted_iota(jnp.int32, (16, columns), 0).astype(F32)
    total = None
    step = 2 if levels % 2 == 0 else 1
    for k0 in range(0, levels, step):
        tents, weights = [], []
        for k in range(k0, k0 + step):
            def row(at):
                return jnp.broadcast_to(rows_ref[at, k, pl.ds(y, 1), :], (16, columns)).astype(BF16)

            zero = jnp.zeros((16, columns), BF16)
            cls, low_hi, low_lo, up_hi, up_lo, joint = [row(at) for at in range(6)]
            feats = [row(at) for at in range(6, 14)]
            tent_hi, tent_lo = [], []
            for c in range(0, CLS, 16):
                here = (spots + float(c)).astype(BF16)
                before = (spots + float(c - 1)).astype(BF16)
                at_low = cls == here
                at_up = cls == before
                tent_hi.append(jnp.where(at_low, low_hi, jnp.where(at_up, up_hi, zero)))
                tent_lo.append(jnp.where(at_low, low_lo, jnp.where(at_up, up_lo, zero)))
            blocks = [[], [], [], []]
            for c in range(0, BT, 16):
                here = (spots + float(c)).astype(BF16)
                before = (spots + float(c - 1)).astype(BF16)
                at_low = joint == here
                at_up = joint == before
                for n, (kind, part) in enumerate(((0, 0), (1, 0), (0, 1), (1, 1))):
                    low = feats[4 * kind + part]
                    up = feats[4 * kind + 2 + part]
                    blocks[n].append(jnp.where(at_low, low, jnp.where(at_up, up, zero)))
            tents.append(jnp.concatenate(tent_hi + tent_lo, 0))
            weights.append(jnp.concatenate(sum(blocks, []), 0))
        product = lax.dot_general(
            jnp.concatenate(tents, 1),
            jnp.concatenate(weights, 1),
            (((1,), (1,)), ((), ())),
            preferred_element_type=F32,
        )
        total = product if total is None else total + product
    total = total[:, :QT] + total[:, QT:]
    return (total[:CLS] + total[CLS:]) * scale


def kernel(
    lon_size,
    zonal_width,
    scale,
    v_ref,
    t_ref,
    bucket_ref,
    slot_ref,
    basin_ref,
    lines_ref,
    numbers_ref,
    depth_ref,
    out_ref,
    rows_ref,
    sums_ref,
    stats_ref,
    part_ref,
    core_ref,
    lons_ref,
    stats_send,
    stats_recv,
    core_send,
    core_recv,
    lon_send,
    lon_recv,
    last_send,
    last_recv,
):
    levels, row_count, columns = v_ref.shape
    chunks = row_count // ROWS
    half = QT * CLS // 2
    lat = lax.axis_index("lat")
    lon = lax.axis_index("lon")
    lev = lax.axis_index("lev")
    other = 1 - lev
    mesh_id = pl.DeviceIdType.MESH

    barrier = pltpu.get_barrier_semaphore()
    pl.semaphore_signal(barrier, inc=1, device_id={"lev": other}, device_id_type=mesh_id)
    for d in range(1, lon_size):
        pl.semaphore_signal(
            barrier, inc=1, device_id={"lon": lax.rem(lon + d, lon_size)}, device_id_type=mesh_id
        )

    basin = basin_ref[...]
    lane = lax.broadcasted_iota(jnp.int32, (row_count, 128), 1)
    packed = jnp.zeros((row_count, 128), F32)
    for b in range(NB):
        mask = (basin == b).astype(F32)
        count = jnp.sum(mask, -1, keepdims=True)
        packed = jnp.where(lane == STATS * levels + b, count, packed)
        for k in range(levels):
            filtered = mask * v_ref[k]
            t = t_ref[k]
            for n, value in enumerate((filtered, mask * t, filtered * t)):
                total = jnp.sum(value, -1, keepdims=True)
                packed = jnp.where(lane == STATS * k + 2 * n + b, total, packed)
    stats_ref[lon] = packed

    pl.semaphore_wait(barrier, lon_size)

    def stats_copy(d):
        return pltpu.make_async_remote_copy(
            src_ref=stats_ref.at[lon],
            dst_ref=stats_ref.at[lon],
            send_sem=stats_send.at[d - 1],
            recv_sem=stats_recv.at[d - 1],
            device_id={"lon": lax.rem(lon + d, lon_size)},
            device_id_type=mesh_id,
        )

    for d in range(1, lon_size):
        stats_copy(d).start()

    numbers = numbers_ref[...]
    spot = (lax.broadcasted_iota(jnp.int32, numbers.shape, 0) == lat) & (
        lax.broadcasted_iota(jnp.int32, numbers.shape, 1) == lon
    )
    own = jnp.sum(jnp.where(spot, numbers.astype(F32), 0.0), -1, keepdims=True)
    own = jnp.sum(own, 0, keepdims=True)
    lines = lines_ref[...]
    square = (row_count, row_count)
    place = lax.broadcasted_iota(jnp.int32, square, 1).astype(F32)
    line = lax.broadcasted_iota(jnp.int32, square, 0)
    hit = jnp.where((line == lines) & (place < own), 1.0, 0.0)
    listed = jnp.max(hit, -1, keepdims=True)
    listed_basin = jnp.where(listed > 0.5, basin, NB)

    for k in range(levels):
        prepare_classes(k, v_ref[k], t_ref[k], bucket_ref[k], slot_ref[k], listed_basin, rows_ref)

    for d in range(1, lon_size):
        stats_copy(d).wait()
    stats = stats_ref[0]
    for n in range(1, lon_size):
        stats = stats + stats_ref[n]

    depth = jnp.zeros((row_count, 128), F32)
    divisors = [
        jnp.maximum(stats[:, STATS * levels + b : STATS * levels + b + 1], 1.0) for b in range(NB)
    ]
    for k in range(levels):
        means = []
        for n in range(2):
            for b in range(NB):
                at = STATS * k + 2 * n + b
                means.append(stats[:, at : at + 1] / divisors[b])
        for b in range(NB):
            at = STATS * k + b
            overturning = stats[:, at : at + 1] * stats[:, at + 2 : at + 3] / divisors[b]
            eddy = (stats[:, at + 4 : at + 5] - overturning) / math.sqrt(zonal_width)
            depth = jnp.where(lane == b * levels + k, overturning, depth)
            depth = jnp.where(lane == (NB + b) * levels + k, eddy, depth)
        prepare_eddies(k, v_ref[k], t_ref[k], listed_basin, means, rows_ref)
    turned = depth.T
    for n in range(2):
        for b in range(NB):
            at = (n * NB + b) * levels
            depth_ref[n, b] = turned[at : at + levels]

    def core_copy(i):
        return pltpu.make_async_remote_copy(
            src_ref=part_ref.at[i, other],
            dst_ref=core_ref.at[i],
            send_sem=core_send.at[i],
            recv_sem=core_recv.at[i],
            device_id={"lev": other},
            device_id_type=mesh_id,
        )

    def lon_copy(i, d):
        return pltpu.make_async_remote_copy(
            src_ref=lons_ref.at[lon, i],
            dst_ref=lons_ref.at[lon, i],
            send_sem=lon_send.at[i, d - 1],
            recv_sem=lon_recv.at[i, d - 1],
            device_id={"lon": lax.rem(lon + d, lon_size)},
            device_id_type=mesh_id,
        )

    def out_block(i):
        rows = pl.ds(pl.multiple_of(i * ROWS, ROWS), ROWS)
        return out_ref.at[rows, pl.ds(pl.multiple_of(lev * half, 128), half)]

    def last_copy(i):
        return pltpu.make_async_remote_copy(
            src_ref=out_block(i),
            dst_ref=out_block(i),
            send_sem=last_send.at[i],
            recv_sem=last_recv.at[i],
            device_id={"lev": other},
            device_id_type=mesh_id,
        )

    def over_cores(i):
        core_copy(i).wait_recv()
        lons_ref[lon, i] = part_ref[i, lev] + core_ref[i]
        for d in range(1, lon_size):
            lon_copy(i, d).start()

    def over_lons(i):
        for d in range(1, lon_size):
            lon_copy(i, d).wait_recv()
        total = lons_ref[0, i]
        for n in range(1, lon_size):
            total = total + lons_ref[n, i]
        out_block(i)[...] = total
        last_copy(i).start()

    def one_chunk(i, carry):
        def one_row(r, inner):
            binned = bin_row(i * ROWS + r, rows_ref, levels, columns, scale)
            binned = jnp.concatenate([binned, jnp.zeros((128 - CLS, QT), F32)], 0)
            sums_ref[pl.ds(r, QT, stride=ROWS), :] = binned.T
            return inner

        lax.fori_loop(0, ROWS, one_row, 0)

        def flatten(group, inner):
            for h in range(2):
                parts = []
                for m in range(4):
                    start = pl.multiple_of((h * (QT // 2) + group * 4 + m) * ROWS, ROWS)
                    parts.append(sums_ref[pl.ds(start, ROWS), :][:, :CLS])
                where = pl.ds(pl.multiple_of(group * (4 * CLS), 128), 4 * CLS)
                part_ref[i, h, :, where] = jnp.concatenate(parts, 1)
            return inner

        lax.fori_loop(0, QT // 8, flatten, 0)
        core_copy(i).start()

        @pl.when(i >= 1)
        def _():
            over_lons(i - 1)

        over_cores(i)
        return carry

    lax.fori_loop(0, chunks, one_chunk, 0)
    over_lons(chunks - 1)

    def finish(i, carry):
        core_copy(i).wait_send()
        for d in range(1, lon_size):
            lon_copy(i, d).wait_send()
        last_copy(i).wait()
        return carry

    lax.fori_loop(0, chunks, finish, 0)


def shards(
    northward_speed,
    thermal_anomaly,
    isopycnal_bucket,
    isopycnal_bucket_slot,
    profile_region_number,
    partition_sea_lines,
    partition_sea_numbers,
):
    levels, row_count, columns = northward_speed.shape
    lon_size = lax.axis_size("lon")
    zonal_width = columns * lon_size
    level_count = levels * lax.axis_size("lev")
    chunks = row_count // ROWS
    half = QT * CLS // 2
    scale = 1.0 / math.sqrt(level_count * zonal_width / (CLS * TCLS))
    vmem = pl.BlockSpec(memory_space=pltpu.VMEM)
    dma = pltpu.SemaphoreType.DMA
    return pl.pallas_call(
        functools.partial(kernel, lon_size, zonal_width, scale),
        out_shape=(
            jax.ShapeDtypeStruct((2, NB, levels, row_count), F32),
            jax.ShapeDtypeStruct((row_count, QT * CLS), F32),
        ),
        in_specs=[vmem] * 7,
        out_specs=(vmem, vmem),
        scratch_shapes=[
            pltpu.VMEM((14, levels, row_count, columns), F32),
            pltpu.VMEM((QT * ROWS, 128), F32),
            pltpu.VMEM((lon_size, row_count, 128), F32),
            pltpu.VMEM((chunks, 2, ROWS, half), F32),
            pltpu.VMEM((chunks, ROWS, half), F32),
            pltpu.VMEM((lon_size, chunks, ROWS, half), F32),
            dma((lon_size - 1,)),
            dma((lon_size - 1,)),
            dma((chunks,)),
            dma((chunks,)),
            dma((chunks, lon_size - 1)),
            dma((chunks, lon_size - 1)),
            dma((chunks,)),
            dma((chunks,)),
        ],
        compiler_params=pltpu.CompilerParams(
            collective_id=0, has_side_effects=True, vmem_limit_bytes=48 * 1024 * 1024
        ),
    )(
        northward_speed,
        thermal_anomaly,
        isopycnal_bucket,
        isopycnal_bucket_slot,
        profile_region_number,
        partition_sea_lines.reshape(1, row_count),
        partition_sea_numbers,
    )


def solution(mesh):
    in_specs = (
        P(("runs", "lev"), "lat", "lon"),
        P(("runs", "lev"), "lat", "lon"),
        P(("runs", "lev"), "lat", "lon"),
        P(("runs", "lev"), "lat", "lon"),
        P(("runs", "lat"), "lon"),
        P(("runs", "lat"), "lon", None),
        P("runs", None),
    )
    out_specs = (P("runs", None, "lev", "lat"), P(("runs", "lat"), None))
    return jax.shard_map(shards, mesh=mesh, in_specs=in_specs, out_specs=out_specs, check_vma=False)
```

time: 132 us -> 79.1 us (0.60)
  waiting for transfers between devices: 42.6 us -> 0 us
  Pallas kernels: 52.4 us -> 69.4 us
  between operations: 14.1 us -> 0.64 us
  blocking collectives: 9.93 us -> 0 us
  other arithmetic: 7.15 us -> 0 us
  local copies, waits for them, and re-layouts: 5.2 us -> 8.78 us
    psum x1 -> x0, waiting for transfers between devices: 42.6 us -> none  [shards(): return (depth_heat, lax.psum(binned, ('lon', 'lev')))]
    pallas_call x1, Pallas kernels: 52.4 us -> 69.4 us  [shards(): pl.pallas_call(functools.partial(kernel, lon_size, zonal_width, scale), o...]
    psum x1 -> x0, blocking collectives: 9.93 us -> none  [shards(): sums, counts = lax.psum((stacked, jnp.sum(masks, -1)), 'lon')]
    unnamed x9 -> x15, local copies, waits for them, and re-layouts: 3.84 us -> 8.78 us
    reduce_sum x2 -> x0, other arithmetic: 3.18 us -> none  [the longest x1 2.03 us: shards(): jnp.sum(filtered, -1)]
  transfers between devices with their start and end apart: 1 -> 0, of which waited for: 1 -> 0; matrix products, arithmetic and copies ran while one was open for 0% -> 0% of each run, Pallas kernels for 0% -> 0%
where the time goes in v2:
time: 79.1 us; the launch traced here: 78.8 us
  Pallas kernels  69.4 us (88%)
  local copies, waits for them, and re-layouts  8.78 us (11%)
    pallas_call x1, Pallas kernels, shards(): pl.pallas_call(functools.partial(kernel, lon_size, zonal_width, scale), o...  69.4 us
    unnamed x15, local copies, waits for them, and re-layouts  8.78 us

profile of v2, /device:TPU:0, one launch (start us, length us, event | category | flops | bytes accessed | tf_op | source)
XLA Modules:
  0.0 78.8 jit_solution(10266674269962015756)
XLA Ops:
  0.6 0.8 copy.9.numbers_ref
  1.4 0.0 copy-start
  1.4 1.2 %copy-done = f32[8,32,896]{2,1,0:T(8,128)S(1)} copy-done((f32[8,32,896]{2,1,0:T(8,128)S(1)}, f32[8,32,896]{2,1,0:T(8,128)}, u32[]{:S(2)}) %copy-start) | copy-done | bytes 917528
  2.6 0.0 copy-start.1
  2.6 1.2 %copy-done.1 = f32[8,32,896]{2,1,0:T(8,128)S(1)} copy-done((f32[8,32,896]{2,1,0:T(8,128)S(1)}, f32[8,32,896]{2,1,0:T(8,128)}, u32[]{:S(2)}) %copy-start.1) | copy-done | bytes 917528
  3.8 0.0 copy-start.2
  3.8 1.2 %copy-done.2 = s32[8,32,896]{2,1,0:T(8,128)S(1)} copy-done((s32[8,32,896]{2,1,0:T(8,128)S(1)}, s32[8,32,896]{2,1,0:T(8,128)}, u32[]{:S(2)}) %copy-start.2) | copy-done | bytes 917528
  4.9 0.0 copy-start.3
  4.9 1.2 %copy-done.3 = f32[8,32,896]{2,1,0:T(8,128)S(1)} copy-done((f32[8,32,896]{2,1,0:T(8,128)S(1)}, f32[8,32,896]{2,1,0:T(8,128)}, u32[]{:S(2)}) %copy-start.3) | copy-done | bytes 917528
  6.1 0.0 copy-start.4
  6.1 0.9 %copy-done.4 = s32[32,896]{1,0:T(8,128)S(1)} copy-done((s32[32,896]{1,0:T(8,128)S(1)}, s32[32,896]{1,0:T(8,128)}, u32[]{:S(2)}) %copy-start.4) | copy-done | bytes 114712
  7.0 0.0 copy-start.5
  7.0 0.7 copy-done.5
  7.7 69.4 %shard_map.86 = (f32[2,2,8,32]{3,2,1,0:T(8,128)S(1)}, f32[32,12288]{1,0:T(8,128)S(1)}) custom-call(f32[8,32,896]{2,1,0:T(8,128)S(1)} %copy-done, f32[8,32,896]{2,1,0:T(8,128)S(1)} %copy-done.1, s32[8,32,896]{2,1,0:T(8,128)S(1)} %copy-done.2, f32[8,32,896]{2,1,0:T(8,128)S(1)} %copy-done.3, s32[32,896]{1,0:T(8,128)S(1)} %copy-done.4, s32[1,32]{1,0:T(1,128)S(1)} %bitcast.1, ...), custom_call_target="tpu_custom_call" | custom-call | tf_op jit(solution)/shard_map/pallas_call | solution.py:330
  77.1 0.6 copy.12
  77.7 1.1 %copy.13 = f32[32,12288]{1,0:T(8,128)} copy(f32[32,12288]{1,0:T(8,128)S(1)} %get-tuple-element.5) | data formatting | bytes 3145728
Async XLA Ops:
  1.4 1.2 %copy-start = (f32[8,32,896]{2,1,0:T(8,128)S(1)}, f32[8,32,896]{2,1,0:T(8,128)}, u32[]{:S(2)}) copy-start(f32[8,32,896]{2,1,0:T(8,128)} %v_ref.1) | copy-start | bytes 2752516
  2.6 1.2 %copy-start.1 = (f32[8,32,896]{2,1,0:T(8,128)S(1)}, f32[8,32,896]{2,1,0:T(8,128)}, u32[]{:S(2)}) copy-start(f32[8,32,896]{2,1,0:T(8,128)} %t_ref.1) | copy-start | bytes 2752516
  3.8 1.2 %copy-start.2 = (s32[8,32,896]{2,1,0:T(8,128)S(1)}, s32[8,32,896]{2,1,0:T(8,128)}, u32[]{:S(2)}) copy-start(s32[8,32,896]{2,1,0:T(8,128)} %bucket_ref.1) | copy-start | bytes 2752516
  4.9 1.2 %copy-start.3 = (f32[8,32,896]{2,1,0:T(8,128)S(1)}, f32[8,32,896]{2,1,0:T(8,128)}, u32[]{:S(2)}) copy-start(f32[8,32,896]{2,1,0:T(8,128)} %slot_ref.1) | copy-start | bytes 2752516
  6.1 0.9 %copy-start.4 = (s32[32,896]{1,0:T(8,128)S(1)}, s32[32,896]{1,0:T(8,128)}, u32[]{:S(2)}) copy-start(s32[32,896]{1,0:T(8,128)} %basin_ref.1) | copy-start | bytes 344068
  7.0 0.7 copy-start.5

commit v3 on v2

--- a/solution.py
+++ b/solution.py
@@ -24,6 +24,7 @@
 
 ROWS = 8
 STATS = 8
+UNROLL = 2
 
 
 def temperature(t):
@@ -88,29 +89,34 @@
             tents.append(jnp.concatenate(tent_hi + tent_lo, 0))
             weights.append(jnp.concatenate(sum(blocks, []), 0))
         product = lax.dot_general(
+            jnp.concatenate(weights, 1),
             jnp.concatenate(tents, 1),
-            jnp.concatenate(weights, 1),
             (((1,), (1,)), ((), ())),
             preferred_element_type=F32,
         )
         total = product if total is None else total + product
-    total = total[:, :QT] + total[:, QT:]
-    return (total[:CLS] + total[CLS:]) * scale
+    total = total[:QT] + total[QT:]
+    return (total[:, :CLS] + total[:, CLS:]) * scale
 
 
 def kernel(
     lon_size,
     zonal_width,
     scale,
+    v_hbm,
+    t_hbm,
+    bucket_hbm,
+    slot_hbm,
+    basin_hbm,
+    lines_ref,
+    numbers_ref,
+    depth_ref,
+    out_ref,
     v_ref,
     t_ref,
     bucket_ref,
     slot_ref,
     basin_ref,
-    lines_ref,
-    numbers_ref,
-    depth_ref,
-    out_ref,
     rows_ref,
     sums_ref,
     stats_ref,
@@ -125,6 +131,9 @@
     lon_recv,
     last_send,
     last_recv,
+    load_sems,
+    done_ref,
+    store_sems,
 ):
     levels, row_count, columns = v_ref.shape
     chunks = row_count // ROWS
@@ -135,6 +144,17 @@
     other = 1 - lev
     mesh_id = pl.DeviceIdType.MESH
 
+    pairs = (
+        (basin_hbm, basin_ref),
+        (v_hbm, v_ref),
+        (t_hbm, t_ref),
+        (bucket_hbm, bucket_ref),
+        (slot_hbm, slot_ref),
+    )
+    loads = [pltpu.make_async_copy(a, b, load_sems.at[n]) for n, (a, b) in enumerate(pairs)]
+    for load in loads:
+        load.start()
+
     barrier = pltpu.get_barrier_semaphore()
     pl.semaphore_signal(barrier, inc=1, device_id={"lev": other}, device_id_type=mesh_id)
     for d in range(1, lon_size):
@@ -142,6 +162,8 @@
             barrier, inc=1, device_id={"lon": lax.rem(lon + d, lon_size)}, device_id_type=mesh_id
         )
 
+    for load in loads[:3]:
+        load.wait()
     basin = basin_ref[...]
     lane = lax.broadcasted_iota(jnp.int32, (row_count, 128), 1)
     packed = jnp.zeros((row_count, 128), F32)
@@ -173,8 +195,8 @@
         stats_copy(d).start()
 
     numbers = numbers_ref[...]
-    spot = (lax.broadcasted_iota(jnp.int32, numbers.shape, 0) == lat) & (
-        lax.broadcasted_iota(jnp.int32, numbers.shape, 1) == lon
+    spot = (lax.broadcasted_iota(jnp.int32, numbers.shape, 0) == lon) & (
+        lax.broadcasted_iota(jnp.int32, numbers.shape, 1) == lat
     )
     own = jnp.sum(jnp.where(spot, numbers.astype(F32), 0.0), -1, keepdims=True)
     own = jnp.sum(own, 0, keepdims=True)
@@ -186,6 +208,8 @@
     listed = jnp.max(hit, -1, keepdims=True)
     listed_basin = jnp.where(listed > 0.5, basin, NB)
 
+    for load in loads[3:]:
+        load.wait()
     for k in range(levels):
         prepare_classes(k, v_ref[k], t_ref[k], bucket_ref[k], slot_ref[k], listed_basin, rows_ref)
 
@@ -240,7 +264,7 @@
 
     def out_block(i):
         rows = pl.ds(pl.multiple_of(i * ROWS, ROWS), ROWS)
-        return out_ref.at[rows, pl.ds(pl.multiple_of(lev * half, 128), half)]
+        return done_ref.at[rows, pl.ds(pl.multiple_of(lev * half, 128), half)]
 
     def last_copy(i):
         return pltpu.make_async_remote_copy(
@@ -252,6 +276,14 @@
             device_id_type=mesh_id,
         )
 
+    def store(i):
+        rows = pl.ds(pl.multiple_of(i * ROWS, ROWS), ROWS)
+        return pltpu.make_async_copy(done_ref.at[rows], out_ref.at[rows], store_sems.at[i])
+
+    def give(i):
+        last_copy(i).wait_recv()
+        store(i).start()
+
     def over_cores(i):
         core_copy(i).wait_recv()
         lons_ref[lon, i] = part_ref[i, lev] + core_ref[i]
@@ -268,26 +300,25 @@
         last_copy(i).start()
 
     def one_chunk(i, carry):
-        def one_row(r, inner):
-            binned = bin_row(i * ROWS + r, rows_ref, levels, columns, scale)
-            binned = jnp.concatenate([binned, jnp.zeros((128 - CLS, QT), F32)], 0)
-            sums_ref[pl.ds(r, QT, stride=ROWS), :] = binned.T
+        def some_rows(step, inner):
+            for u in range(UNROLL):
+                r = step * UNROLL + u
+                binned = bin_row(i * ROWS + r, rows_ref, levels, columns, scale)
+                binned = jnp.concatenate([binned, jnp.zeros((QT, 128 - CLS), F32)], 1)
+                sums_ref[pl.ds(r, QT, stride=ROWS), :] = binned
             return inner
 
-        lax.fori_loop(0, ROWS, one_row, 0)
-
-        def flatten(group, inner):
-            for h in range(2):
-                parts = []
-                for m in range(4):
-                    start = pl.multiple_of((h * (QT // 2) + group * 4 + m) * ROWS, ROWS)
-                    parts.append(sums_ref[pl.ds(start, ROWS), :][:, :CLS])
-                where = pl.ds(pl.multiple_of(group * (4 * CLS), 128), 4 * CLS)
-                part_ref[i, h, :, where] = jnp.concatenate(parts, 1)
-            return inner
-
-        lax.fori_loop(0, QT // 8, flatten, 0)
+        lax.fori_loop(0, ROWS // UNROLL, some_rows, 0)
+
+        for m in range(0, QT, 4):
+            parts = [sums_ref[(m + n) * ROWS : (m + n + 1) * ROWS, :][:, :CLS] for n in range(4)]
+            h, at = divmod(m * CLS, half)
+            part_ref[i, h, :, at : at + 4 * CLS] = jnp.concatenate(parts, 1)
         core_copy(i).start()
+
+        @pl.when(i >= 2)
+        def _():
+            give(i - 2)
 
         @pl.when(i >= 1)
         def _():
@@ -297,13 +328,17 @@
         return carry
 
     lax.fori_loop(0, chunks, one_chunk, 0)
+    if chunks >= 2:
+        give(chunks - 2)
     over_lons(chunks - 1)
+    give(chunks - 1)
 
     def finish(i, carry):
         core_copy(i).wait_send()
         for d in range(1, lon_size):
             lon_copy(i, d).wait_send()
-        last_copy(i).wait()
+        last_copy(i).wait_send()
+        store(i).wait()
         return carry
 
     lax.fori_loop(0, chunks, finish, 0)
@@ -333,9 +368,14 @@
             jax.ShapeDtypeStruct((2, NB, levels, row_count), F32),
             jax.ShapeDtypeStruct((row_count, QT * CLS), F32),
         ),
-        in_specs=[vmem] * 7,
-        out_specs=(vmem, vmem),
+        in_specs=[pl.BlockSpec(memory_space=pl.ANY)] * 5 + [vmem] * 2,
+        out_specs=(vmem, pl.BlockSpec(memory_space=pl.ANY)),
         scratch_shapes=[
+            pltpu.VMEM((levels, row_count, columns), F32),
+            pltpu.VMEM((levels, row_count, columns), F32),
+            pltpu.VMEM((levels, row_count, columns), jnp.int32),
+            pltpu.VMEM((levels, row_count, columns), F32),
+            pltpu.VMEM((row_count, columns), jnp.int32),
             pltpu.VMEM((14, levels, row_count, columns), F32),
             pltpu.VMEM((QT * ROWS, 128), F32),
             pltpu.VMEM((lon_size, row_count, 128), F32),
@@ -350,9 +390,12 @@
             dma((chunks, lon_size - 1)),
             dma((chunks,)),
             dma((chunks,)),
+            dma((5,)),
+            pltpu.VMEM((row_count, QT * CLS), F32),
+            dma((chunks,)),
         ],
         compiler_params=pltpu.CompilerParams(
-            collective_id=0, has_side_effects=True, vmem_limit_bytes=48 * 1024 * 1024
+            collective_id=0, has_side_effects=True, vmem_limit_bytes=60 * 1024 * 1024
         ),
     )(
         northward_speed,
@@ -361,7 +404,7 @@
         isopycnal_bucket_slot,
         profile_region_number,
         partition_sea_lines.reshape(1, row_count),
-        partition_sea_numbers,
+        partition_sea_numbers.T,
     )
 
 

time: 79.1 us -> 62.6 us (0.79)
  Pallas kernels: 69.4 us -> 57.1 us
  local copies, waits for them, and re-layouts: 8.78 us -> 3.98 us
    pallas_call x1, Pallas kernels: 69.4 us -> 57.1 us  [shards(): pl.pallas_call(functools.partial(kernel, lon_size, zonal_width, scale), o...]
    unnamed x15 -> x2, local copies, waits for them, and re-layouts: 8.78 us -> 3.98 us
where the time goes in v3:
time: 62.6 us; the launch traced here: 61.7 us
  Pallas kernels  57.1 us (91%)
  local copies, waits for them, and re-layouts  3.98 us (6%)
  between operations  0.64 us (1%)
    pallas_call x1, Pallas kernels, shards(): pl.pallas_call(functools.partial(kernel, lon_size, zonal_width, scale), o...  57.1 us
    unnamed x2, local copies, waits for them, and re-layouts  3.98 us

profile of v3, /device:TPU:0, one launch (start us, length us, event | category | flops | bytes accessed | tf_op | source)
XLA Modules:
  0.0 61.7 jit_solution(4886199446790539839)
XLA Ops:
  0.6 57.1 %shard_map.86 = (f32[2,2,8,32]{3,2,1,0:T(8,128)}, f32[32,12288]{1,0:T(8,128)}) custom-call(f32[8,32,896]{2,1,0:T(8,128)} %v_hbm.1, f32[8,32,896]{2,1,0:T(8,128)} %t_hbm.1, s32[8,32,896]{2,1,0:T(8,128)} %bucket_hbm.1, f32[8,32,896]{2,1,0:T(8,128)} %slot_hbm.1, s32[32,896]{1,0:T(8,128)} %basin_hbm.1, s32[1,32]{1,0:T(1,128)} %bitcast.3, s32[2,4]{1,0:T(2,128)} %bitcast.2), custom_call_target="tpu_custom_call" | custom-call | tf_op jit(solution)/shard_map/pallas_call | solution.py:365
  57.7 1.3 %copy.11 = f32[2,2,8,32]{3,2,1,0:T(8,128)} copy(f32[2,2,8,32]{3,2,1,0:T(8,128)} %get-tuple-element.4) | data formatting | bytes 8192
  59.0 2.7 %copy.12 = f32[32,12288]{1,0:T(8,128)} copy(f32[32,12288]{1,0:T(8,128)} %get-tuple-element.5) | data formatting | bytes 3145728

commit v4 on v3

--- a/solution.py
+++ b/solution.py
@@ -24,7 +24,8 @@
 
 ROWS = 8
 STATS = 8
-UNROLL = 2
+UNROLL = 4
+PIECES = 4
 
 
 def temperature(t):
@@ -132,8 +133,6 @@
     last_send,
     last_recv,
     load_sems,
-    done_ref,
-    store_sems,
 ):
     levels, row_count, columns = v_ref.shape
     chunks = row_count // ROWS
@@ -242,62 +241,62 @@
             at = (n * NB + b) * levels
             depth_ref[n, b] = turned[at : at + levels]
 
-    def core_copy(i):
+    width = half // PIECES
+
+    def core_copy(i, p):
+        lanes = pl.ds(p * width, width)
         return pltpu.make_async_remote_copy(
-            src_ref=part_ref.at[i, other],
-            dst_ref=core_ref.at[i],
-            send_sem=core_send.at[i],
-            recv_sem=core_recv.at[i],
+            src_ref=part_ref.at[i, other, :, lanes],
+            dst_ref=core_ref.at[i, :, lanes],
+            send_sem=core_send.at[i, p],
+            recv_sem=core_recv.at[i, p],
             device_id={"lev": other},
             device_id_type=mesh_id,
         )
 
-    def lon_copy(i, d):
+    def lon_copy(i, p, d):
+        block = lons_ref.at[lon, i, :, pl.ds(p * width, width)]
         return pltpu.make_async_remote_copy(
-            src_ref=lons_ref.at[lon, i],
-            dst_ref=lons_ref.at[lon, i],
-            send_sem=lon_send.at[i, d - 1],
-            recv_sem=lon_recv.at[i, d - 1],
+            src_ref=block,
+            dst_ref=block,
+            send_sem=lon_send.at[i, p, d - 1],
+            recv_sem=lon_recv.at[i, p, d - 1],
             device_id={"lon": lax.rem(lon + d, lon_size)},
             device_id_type=mesh_id,
         )
 
-    def out_block(i):
+    def out_block(i, p):
         rows = pl.ds(pl.multiple_of(i * ROWS, ROWS), ROWS)
-        return done_ref.at[rows, pl.ds(pl.multiple_of(lev * half, 128), half)]
-
-    def last_copy(i):
+        return out_ref.at[rows, pl.ds(pl.multiple_of(lev * half + p * width, 128), width)]
+
+    def last_copy(i, p):
         return pltpu.make_async_remote_copy(
-            src_ref=out_block(i),
-            dst_ref=out_block(i),
-            send_sem=last_send.at[i],
-            recv_sem=last_recv.at[i],
+            src_ref=out_block(i, p),
+            dst_ref=out_block(i, p),
+            send_sem=last_send.at[i, p],
+            recv_sem=last_recv.at[i, p],
             device_id={"lev": other},
             device_id_type=mesh_id,
         )
 
-    def store(i):
-        rows = pl.ds(pl.multiple_of(i * ROWS, ROWS), ROWS)
-        return pltpu.make_async_copy(done_ref.at[rows], out_ref.at[rows], store_sems.at[i])
-
-    def give(i):
-        last_copy(i).wait_recv()
-        store(i).start()
-
     def over_cores(i):
-        core_copy(i).wait_recv()
-        lons_ref[lon, i] = part_ref[i, lev] + core_ref[i]
-        for d in range(1, lon_size):
-            lon_copy(i, d).start()
+        for p in range(PIECES):
+            lanes = slice(p * width, (p + 1) * width)
+            core_copy(i, p).wait_recv()
+            lons_ref[lon, i, :, lanes] = part_ref[i, lev, :, lanes] + core_ref[i, :, lanes]
+            for d in range(1, lon_size):
+                lon_copy(i, p, d).start()
 
     def over_lons(i):
-        for d in range(1, lon_size):
-            lon_copy(i, d).wait_recv()
-        total = lons_ref[0, i]
-        for n in range(1, lon_size):
-            total = total + lons_ref[n, i]
-        out_block(i)[...] = total
-        last_copy(i).start()
+        for p in range(PIECES):
+            lanes = slice(p * width, (p + 1) * width)
+            for d in range(1, lon_size):
+                lon_copy(i, p, d).wait_recv()
+            total = lons_ref[0, i, :, lanes]
+            for n in range(1, lon_size):
+                total = total + lons_ref[n, i, :, lanes]
+            out_block(i, p)[...] = total
+            last_copy(i, p).start()
 
     def one_chunk(i, carry):
         def some_rows(step, inner):
@@ -310,15 +309,16 @@
 
         lax.fori_loop(0, ROWS // UNROLL, some_rows, 0)
 
-        for m in range(0, QT, 4):
-            parts = [sums_ref[(m + n) * ROWS : (m + n + 1) * ROWS, :][:, :CLS] for n in range(4)]
-            h, at = divmod(m * CLS, half)
-            part_ref[i, h, :, at : at + 4 * CLS] = jnp.concatenate(parts, 1)
-        core_copy(i).start()
-
-        @pl.when(i >= 2)
-        def _():
-            give(i - 2)
+        for p in range(PIECES):
+            for h in range(2):
+                for m in range(p * (QT // 2 // PIECES), (p + 1) * (QT // 2 // PIECES), 4):
+                    first = (h * (QT // 2) + m) * ROWS
+                    parts = [
+                        sums_ref[first + n * ROWS : first + (n + 1) * ROWS, :][:, :CLS]
+                        for n in range(4)
+                    ]
+                    part_ref[i, h, :, m * CLS : (m + 4) * CLS] = jnp.concatenate(parts, 1)
+            core_copy(i, p).start()
 
         @pl.when(i >= 1)
         def _():
@@ -328,17 +328,14 @@
         return carry
 
     lax.fori_loop(0, chunks, one_chunk, 0)
-    if chunks >= 2:
-        give(chunks - 2)
     over_lons(chunks - 1)
-    give(chunks - 1)
 
     def finish(i, carry):
-        core_copy(i).wait_send()
-        for d in range(1, lon_size):
-            lon_copy(i, d).wait_send()
-        last_copy(i).wait_send()
-        store(i).wait()
+        for p in range(PIECES):
+            core_copy(i, p).wait_send()
+            for d in range(1, lon_size):
+                lon_copy(i, p, d).wait_send()
+            last_copy(i, p).wait()
         return carry
 
     lax.fori_loop(0, chunks, finish, 0)
@@ -365,11 +362,11 @@
     return pl.pallas_call(
         functools.partial(kernel, lon_size, zonal_width, scale),
         out_shape=(
-            jax.ShapeDtypeStruct((2, NB, levels, row_count), F32),
-            jax.ShapeDtypeStruct((row_count, QT * CLS), F32),
+            pltpu.VMEM((2, NB, levels, row_count), F32),
+            pltpu.VMEM((row_count, QT * CLS), F32),
         ),
         in_specs=[pl.BlockSpec(memory_space=pl.ANY)] * 5 + [vmem] * 2,
-        out_specs=(vmem, pl.BlockSpec(memory_space=pl.ANY)),
+        out_specs=(vmem, vmem),
         scratch_shapes=[
             pltpu.VMEM((levels, row_count, columns), F32),
             pltpu.VMEM((levels, row_count, columns), F32),
@@ -384,15 +381,13 @@
             pltpu.VMEM((lon_size, chunks, ROWS, half), F32),
             dma((lon_size - 1,)),
             dma((lon_size - 1,)),
-            dma((chunks,)),
-            dma((chunks,)),
-            dma((chunks, lon_size - 1)),
-            dma((chunks, lon_size - 1)),
-            dma((chunks,)),
-            dma((chunks,)),
+            dma((chunks, PIECES)),
+            dma((chunks, PIECES)),
+            dma((chunks, PIECES, lon_size - 1)),
+            dma((chunks, PIECES, lon_size - 1)),
+            dma((chunks, PIECES)),
+            dma((chunks, PIECES)),
             dma((5,)),
-            pltpu.VMEM((row_count, QT * CLS), F32),
-            dma((chunks,)),
         ],
         compiler_params=pltpu.CompilerParams(
             collective_id=0, has_side_effects=True, vmem_limit_bytes=60 * 1024 * 1024

time: 62.6 us -> 57.4 us (0.917); the launches traced: 61.7 us -> 57.2 us
  Pallas kernels: 57.1 us -> 54.8 us
  local copies, waits for them, and re-layouts: 3.98 us -> 1.75 us
    pallas_call x1, Pallas kernels: 57.1 us -> 54.8 us  [shards(): pl.pallas_call(functools.partial(kernel, lon_size, zonal_width, scale), o...]
    unnamed x2, local copies, waits for them, and re-layouts: 3.98 us -> 1.75 us
where the time goes in v4:
time: 57.4 us; the launch traced here: 57.2 us
  Pallas kernels  54.8 us (95%)
  local copies, waits for them, and re-layouts  1.75 us (3%)
  between operations  0.64 us (1%)
    pallas_call x1, Pallas kernels, shards(): pl.pallas_call(functools.partial(kernel, lon_size, zonal_width, scale), o...  54.8 us
    unnamed x2, local copies, waits for them, and re-layouts  1.75 us

profile of v4, /device:TPU:0, one launch (start us, length us, event | category | flops | bytes accessed | tf_op | source)
XLA Modules:
  0.0 57.2 jit_solution(14289325554382535387)
XLA Ops:
  0.6 54.8 %shard_map.86 = (f32[2,2,8,32]{3,2,1,0:T(8,128)S(1)}, f32[32,12288]{1,0:T(8,128)S(1)}) custom-call(f32[8,32,896]{2,1,0:T(8,128)} %v_hbm.1, f32[8,32,896]{2,1,0:T(8,128)} %t_hbm.1, s32[8,32,896]{2,1,0:T(8,128)} %bucket_hbm.1, f32[8,32,896]{2,1,0:T(8,128)} %slot_hbm.1, s32[32,896]{1,0:T(8,128)} %basin_hbm.1, s32[1,32]{1,0:T(1,128)} %bitcast.3, s32[2,4]{1,0:T(2,128)} %bitcast.2), custom_call_target="tpu_custom_call" | custom-call | tf_op jit(solution)/shard_map/pallas_call | solution.py:362
  55.4 0.6 %copy.11 = f32[2,2,8,32]{3,2,1,0:T(8,128)} copy(f32[2,2,8,32]{3,2,1,0:T(8,128)S(1)} %get-tuple-element.2) | data formatting | bytes 8192
  56.0 1.1 %copy.12 = f32[32,12288]{1,0:T(8,128)} copy(f32[32,12288]{1,0:T(8,128)S(1)} %get-tuple-element.3) | data formatting | bytes 3145728

commit v5 on v4

--- a/solution.py
+++ b/solution.py
@@ -24,7 +24,7 @@
 
 ROWS = 8
 STATS = 8
-UNROLL = 4
+UNROLL = 8
 PIECES = 4
 
 

time: 57.4 us -> 56.2 us (0.979)
  Pallas kernels: 54.8 us -> 53.6 us
    pallas_call x1, Pallas kernels: 54.8 us -> 53.6 us  [shards(): pl.pallas_call(functools.partial(kernel, lon_size, zonal_width, scale), o...]
where the time goes in v5:
time: 56.2 us; the launch traced here: 56 us
  Pallas kernels  53.6 us (95%)
  local copies, waits for them, and re-layouts  1.75 us (3%)
  between operations  0.64 us (1%)
    pallas_call x1, Pallas kernels, shards(): pl.pallas_call(functools.partial(kernel, lon_size, zonal_width, scale), o...  53.6 us
    unnamed x2, local copies, waits for them, and re-layouts  1.75 us

profile of v5, /device:TPU:0, one launch (start us, length us, event | category | flops | bytes accessed | tf_op | source)
XLA Modules:
  0.0 56.0 jit_solution(3762446749467449724)
XLA Ops:
  0.6 53.6 %shard_map.86 = (f32[2,2,8,32]{3,2,1,0:T(8,128)S(1)}, f32[32,12288]{1,0:T(8,128)S(1)}) custom-call(f32[8,32,896]{2,1,0:T(8,128)} %v_hbm.1, f32[8,32,896]{2,1,0:T(8,128)} %t_hbm.1, s32[8,32,896]{2,1,0:T(8,128)} %bucket_hbm.1, f32[8,32,896]{2,1,0:T(8,128)} %slot_hbm.1, s32[32,896]{1,0:T(8,128)} %basin_hbm.1, s32[1,32]{1,0:T(1,128)} %bitcast.3, s32[2,4]{1,0:T(2,128)} %bitcast.2), custom_call_target="tpu_custom_call" | custom-call | tf_op jit(solution)/shard_map/pallas_call | solution.py:362
  54.3 0.6 %copy.11 = f32[2,2,8,32]{3,2,1,0:T(8,128)} copy(f32[2,2,8,32]{3,2,1,0:T(8,128)S(1)} %get-tuple-element.2) | data formatting | bytes 8192
  54.9 1.1 %copy.12 = f32[32,12288]{1,0:T(8,128)} copy(f32[32,12288]{1,0:T(8,128)S(1)} %get-tuple-element.3) | data formatting | bytes 3145728
